TPU v7x, 32 devices: a whole 2x2x4 slice. The times are simulated.
32 devices in a mesh: tr: 4 (over x, core), gz: 8 (over z, y).
Axes of the slice: x: 2, y: 2, z: 4, core: 2. Of those that a mesh axis runs over, the one named last changes fastest.
Arguments:
- tokens: bfloat16 [40, 32, 8, 768], P('gz', None, 'tr'), may hold values from -6 to 6
- cotangent: bfloat16 [40, 32, 8, 768], P('gz', None, 'tr'), may hold values from -6 to 6
- gain_x: float32 [768], replicated, may hold values from 0.1 to 1.9
- wqkv_x: bfloat16 [768, 2304], P('tr'), as said below
- wo_x: bfloat16 [768, 768], P('tr'), may hold values from -0.21875 to 0.21875
- gain_z: float32 [768], replicated, may hold values from 0.1 to 1.9
- wqkv_z: bfloat16 [768, 2304], P('tr'), as said below
- wo_z: bfloat16 [768, 768], P('tr'), may hold values from -0.21875 to 0.21875
Outputs:
- grad_tokens: bfloat16 [40, 32, 8, 768], P('gz', None, 'tr')
Inputs may be any that keep to these rules, and one draw needn't show every extreme that they name: `wqkv_x`: query, key and value columns side by side, each block split into 6 heads of 128. `wqkv_z`: query, key and value columns side by side, each block split into 6 heads of 128.
All inputs are finite; a program needn't handle non-finite values.
Results may differ from a plain program's by a relative error of at most 0.038.
The roundings to bfloat16 on the way count: a program that leaves them out, or rounds other values in their place, can miss the bound.
Values may be sent and summed in bfloat16 or wider, within the bound.
A program may use at most 64 MiB of HBM per device.

v0:
```python
import math
import jax
import jax.numpy as jnp
from jax import lax
from jax.sharding import PartitionSpec as P

H = 6


def head_split(packed, index, model_width):
    piece = packed[..., index * model_width : (index + 1) * model_width]
    return piece.reshape(piece.shape[:-1] + (H, model_width // H))


def merge_heads(value):
    return value.reshape(value.shape[:-2] + (value.shape[-2] * value.shape[-1],))


def recompute(tokens_in, gain_vec, w_in, layout):
    model_width = w_in.shape[0]
    factor = 1.0 / math.sqrt(model_width // H)
    widened = tokens_in.astype(jnp.float32)
    inv_rms = lax.rsqrt(jnp.mean(widened * widened, axis=-1, keepdims=True) + 1e-06)
    normed = (widened * inv_rms * gain_vec).astype(jnp.bfloat16)
    packed = jnp.dot(normed, w_in, preferred_element_type=jnp.float32).astype(jnp.bfloat16)
    queries = head_split(packed, 0, model_width)
    key_part = head_split(packed, 1, model_width)
    values = head_split(packed, 2, model_width)
    key_form = layout.replace("l", "m")
    scores = (
        jnp.einsum(
            layout + "," + key_form + "->bhlm",
            queries,
            key_part,
            preferred_element_type=jnp.float32,
        )
        * factor
    )
    highest = jnp.max(scores, axis=-1, keepdims=True)
    expanded = jnp.exp(scores - highest)
    probs = expanded / jnp.sum(expanded, axis=-1, keepdims=True)
    return (widened, inv_rms, queries, key_part, values, probs, probs.astype(jnp.bfloat16), factor)


def forward_out(tokens_in, gain_vec, w_in, w_out, layout):
    widened, inv_rms, queries, key_part, values, probs, probs_b, factor = recompute(
        tokens_in, gain_vec, w_in, layout
    )
    key_form = layout.replace("l", "m")
    mixed = jnp.einsum(
        "bhlm," + key_form + "->" + layout, probs_b, values, preferred_element_type=jnp.float32
    )
    mixed = merge_heads(mixed.astype(jnp.bfloat16))
    return (widened + jnp.dot(mixed, w_out, preferred_element_type=jnp.float32)).astype(
        jnp.bfloat16
    )


def backward(tokens_in, upstream, gain_vec, w_in, w_out, layout):
    widened, inv_rms, queries, key_part, values, probs, probs_b, factor = recompute(
        tokens_in, gain_vec, w_in, layout
    )
    key_form = layout.replace("l", "m")
    d_mixed = jnp.dot(upstream, w_out.T, preferred_element_type=jnp.float32).astype(jnp.bfloat16)
    d_mixed = d_mixed.reshape(d_mixed.shape[:-1] + (H, d_mixed.shape[-1] // H))
    d_probs = jnp.einsum(
        layout + "," + key_form + "->bhlm", d_mixed, values, preferred_element_type=jnp.float32
    )
    d_values = jnp.einsum(
        "bhlm," + layout + "->" + key_form, probs_b, d_mixed, preferred_element_type=jnp.float32
    ).astype(jnp.bfloat16)
    centre = jnp.sum(probs * d_probs, axis=-1, keepdims=True)
    d_scores = (probs * (d_probs - centre) * factor).astype(jnp.bfloat16)
    d_queries = jnp.einsum(
        "bhlm," + key_form + "->" + layout, d_scores, key_part, preferred_element_type=jnp.float32
    ).astype(jnp.bfloat16)
    d_keys = jnp.einsum(
        "bhlm," + layout + "->" + key_form, d_scores, queries, preferred_element_type=jnp.float32
    ).astype(jnp.bfloat16)
    joined = jnp.concatenate(
        [merge_heads(d_queries), merge_heads(d_keys), merge_heads(d_values)], axis=-1
    )
    d_normed = jnp.dot(joined, w_in.T, preferred_element_type=jnp.float32)
    scaled = d_normed * gain_vec
    d_tokens = inv_rms * (
        scaled - widened * inv_rms * inv_rms * jnp.mean(scaled * widened, axis=-1, keepdims=True)
    )
    return (upstream.astype(jnp.float32) + d_tokens).astype(jnp.bfloat16)


def line_forward(lines, gain_vec, w_in, w_out):
    feature_count = lines.shape[3]
    flat = lines.reshape(-1, lines.shape[2], feature_count)
    return forward_out(flat, gain_vec, w_in, w_out, "blhe").reshape(lines.shape)


def line_backward(lines, upstream, gain_vec, w_in, w_out):
    feature_count = lines.shape[3]
    flat = lines.reshape(-1, lines.shape[2], feature_count)
    flat_up = upstream.reshape(flat.shape)
    return backward(flat, flat_up, gain_vec, w_in, w_out, "blhe").reshape(lines.shape)


def per_device(tokens, cotangent, gain_x, wqkv_x, wo_x, gain_z, wqkv_z, wo_z):
    full_in_x, full_out_x = (
        lax.all_gather(wqkv_x, "tr", axis=0, tiled=True),
        lax.all_gather(wo_x, "tr", axis=0, tiled=True),
    )
    full_in_z, full_out_z = (
        lax.all_gather(wqkv_z, "tr", axis=0, tiled=True),
        lax.all_gather(wo_z, "tr", axis=0, tiled=True),
    )
    width = tokens.shape[-1]
    lines = lax.all_to_all(tokens, "tr", split_axis=1, concat_axis=2, tiled=True)
    cot_lines = lax.all_to_all(cotangent, "tr", split_axis=1, concat_axis=2, tiled=True)
    cells = lines.shape[1] * lines.shape[2]
    flat = (lines.shape[0], cells, width)
    cot_columns = lax.all_to_all(
        cot_lines.reshape(flat), "gz", split_axis=1, concat_axis=0, tiled=True
    )
    mid_lines = line_forward(lines, gain_x, full_in_x, full_out_x)
    mid_columns = lax.all_to_all(
        mid_lines.reshape(flat), "gz", split_axis=1, concat_axis=0, tiled=True
    )
    grad_columns = backward(mid_columns, cot_columns, gain_z, full_in_z, full_out_z, "lbhe")
    grad_lines = lax.all_to_all(grad_columns, "gz", split_axis=0, concat_axis=1, tiled=True)
    result_lines = line_backward(
        lines, grad_lines.reshape(lines.shape), gain_x, full_in_x, full_out_x
    )
    return lax.all_to_all(result_lines, "tr", split_axis=2, concat_axis=1, tiled=True)


def solution(mesh):
    return jax.shard_map(
        per_device,
        mesh=mesh,
        in_specs=(
            P("gz", None, "tr", None),
            P("gz", None, "tr", None),
            P(),
            P("tr", None),
            P("tr", None),
            P(),
            P("tr", None),
            P("tr", None),
        ),
        out_specs=P("gz", None, "tr", None),
        check_vma=False,
    )
```

profile of v0, /device:TPU:0, one launch (start us, length us, event | category | flops | bytes accessed | tf_op | source)
XLA Modules:
  0.0 194.4 jit_solution(14103475853062895245)
XLA Ops:
  6.5 0.7 all-gather.5.cloned.1.call-update
  7.3 0.7 all-gather.7.cloned.1.call-update
  8.1 0.7 all-gather.11.cloned.1.call-update
  8.8 0.5 all-gather.9.cloned.1.call-update
  9.3 1.1 copy.114
  10.5 4.2 %all-to-all-start.2 = ((bf16[5,32,2,768]{3,2,0,1:T(2,128)(2,1)}), bf16[5,32,2,768]{3,2,0,1:T(2,128)(2,1)S(1)}, u32[]{:S(2)}, u32[]{:S(2)}) async-start(bf16[5,32,2,768]{3,2,0,1:T(2,128)(2,1)} %copy.114), calls=%async_computation.2 | async-start | bytes 983040 | tf_op jit(solution)/shard_map/all_to_all | solution.py:114
  14.7 1.1 copy.109
  15.8 9.2 %all-to-all-done.2 = bf16[5,32,2,768]{3,2,0,1:T(2,128)(2,1)S(1)} async-done(((bf16[5,32,2,768]{3,2,0,1:T(2,128)(2,1)}), bf16[5,32,2,768]{3,2,0,1:T(2,128)(2,1)S(1)}, u32[]{:S(2)}, u32[]{:S(2)}) %all-to-all-start.2) | async-done | bytes 491552 | tf_op jit(solution)/shard_map/all_to_all | solution.py:114
  25.0 3.5 %all-to-all-start = ((bf16[5,32,2,768]{3,2,0,1:T(2,128)(2,1)}), bf16[5,32,2,768]{3,2,0,1:T(2,128)(2,1)S(1)}, u32[]{:S(2)}, u32[]{:S(2)}) async-start(bf16[5,32,2,768]{3,2,0,1:T(2,128)(2,1)} %copy.109), calls=%async_computation | async-start | bytes 983040 | tf_op jit(solution)/shard_map/all_to_all | solution.py:115
  28.4 0.6 multiply_reduce_fusion.4
  29.4 13.1 %all-to-all-done = bf16[5,32,2,768]{3,2,0,1:T(2,128)(2,1)S(1)} async-done(((bf16[5,32,2,768]{3,2,0,1:T(2,128)(2,1)}), bf16[5,32,2,768]{3,2,0,1:T(2,128)(2,1)S(1)}, u32[]{:S(2)}, u32[]{:S(2)}) %all-to-all-start) | async-done | bytes 491552 | tf_op jit(solution)/shard_map/all_to_all | solution.py:115
  42.5 1.0 copy.144
  43.5 7.3 %all-to-all-start.1 = ((bf16[5,64,768]{2,0,1:T(8,128)(2,1)}), bf16[5,64,768]{2,0,1:T(8,128)(2,1)S(1)}, u32[]{:S(2)}, u32[]{:S(2)}) async-start(bf16[5,64,768]{2,0,1:T(8,128)(2,1)} %bitcast.2), calls=%async_computation.1 | async-start | bytes 1572864 | tf_op jit(solution)/shard_map/all_to_all | solution.py:118
  50.8 0.4 copy_bitcast_fusion
  51.2 0.7 reshape.140
  51.9 3.4 %convolution_convert_fusion.1 = bf16[40,8,2304]{2,1,0:T(8,128)(2,1)S(1)} fusion(bf16[768,2304]{1,0:T(8,128)(2,1)} %all-gather.5.cloned.1.call-done, f32[40,8,768]{2,1,0:T(8,128)S(1)} %reshape.140, f32[768]{0:T(1024)S(1)} %copy-done.8, f32[40,8]{1,0:T(8,128)S(1)} %copy.119), kind=kOutput, calls=%fused_computation.5 | convolution fusion | flops 1133936640 | bytes 6000896 | tf_op jit(solution)/shard_map/dot_general | solution.py:25
  55.3 1.8 fusion.105
  57.1 11.9 %all-gather.7.cloned.1.call-done = bf16[768,768]{1,0:T(8,128)(2,1)} async-done(((bf16[192,768]{1,0:T(8,128)(2,1)}), bf16[768,768]{1,0:T(8,128)(2,1)}) %all-gather.7.cloned.1.call-update) | async-done | bytes 1179664 | tf_op jit(solution)/shard_map/all_gather | solution.py:107
  69.0 2.6 %fusion.40 = bf16[40,8,768]{2,1,0:T(8,128)(2,1)S(1)} fusion(f32[40,8,768]{2,1,0:T(8,128)S(1)} %reshape.140, bf16[768,768]{1,0:T(8,128)(2,1)} %all-gather.7.cloned.1.call-done, bf16[40,8,2304]{2,1,0:T(8,128)(2,1)} %copy-done.5, f32[40,6,8,8]{2,3,1,0:T(8,128)} %get-tuple-element.9, f32[40,6,8]{2,1,0:T(8,128)S(1)} %get-tuple-element.8), kind=kOutput, calls=%fused_computation.38 | convolution fusion | flops 382187520 | bytes 4136448 | tf_op jit(solution)/shard_map/dot_general | solution.py:54
  71.7 1.2 copy.121
  72.9 5.5 %all-to-all-start.3 = ((bf16[5,64,768]{2,0,1:T(8,128)(2,1)}), bf16[5,64,768]{2,0,1:T(8,128)(2,1)S(1)}, u32[]{:S(2)}, u32[]{:S(2)}) async-start(bf16[5,64,768]{2,0,1:T(8,128)(2,1)} %copy.121), calls=%async_computation.3 | async-start | bytes 1572864 | tf_op jit(solution)/shard_map/all_to_all | solution.py:122
  78.5 9.5 %all-gather.11.cloned.1.call-done = bf16[768,768]{1,0:T(8,128)(2,1)} async-done(((bf16[192,768]{1,0:T(8,128)(2,1)}), bf16[768,768]{1,0:T(8,128)(2,1)}) %all-gather.11.cloned.1.call-update) | async-done | bytes 1179664 | tf_op jit(solution)/shard_map/all_gather | solution.py:111
  88.1 2.6 %fusion.43 = bf16[40,8,6,128]{3,1,2,0:T(8,128)(2,1)} fusion(bf16[40,8,768]{2,1,0:T(8,128)(2,1)S(1)} %bitcast.138, bf16[768,768]{1,0:T(8,128)(2,1)} %all-gather.11.cloned.1.call-done), kind=kOutput, calls=%fused_computation.50 | convolution fusion | flops 377733120 | bytes 2162688 | tf_op jit(solution)/shard_map/dot_general | solution.py:64
  90.7 8.3 %all-to-all-done.3 = bf16[5,64,768]{2,0,1:T(8,128)(2,1)S(1)} async-done(((bf16[5,64,768]{2,0,1:T(8,128)(2,1)}), bf16[5,64,768]{2,0,1:T(8,128)(2,1)S(1)}, u32[]{:S(2)}, u32[]{:S(2)}) %all-to-all-start.3) | async-done | bytes 491552 | tf_op jit(solution)/shard_map/all_to_all | solution.py:122
  99.0 0.3 multiply_reduce_fusion
  99.6 20.7 %all-gather.9.cloned.1.call-done = bf16[768,2304]{1,0:T(8,128)(2,1)} async-done(((bf16[192,2304]{1,0:T(8,128)(2,1)}), bf16[768,2304]{1,0:T(8,128)(2,1)}) %all-gather.9.cloned.1.call-update) | async-done | bytes 3538960 | tf_op jit(solution)/shard_map/all_gather | solution.py:110
  120.3 3.3 %convolution_convert_fusion = bf16[40,8,2304]{2,1,0:T(8,128)(2,1)S(1)} fusion(bf16[768,2304]{1,0:T(8,128)(2,1)} %all-gather.9.cloned.1.call-done, f32[40,8,768]{2,1,0:T(8,128)S(1)} %bitcast.135, f32[768]{0:T(1024)S(1)} %copy-done.7, f32[40,8]{1,0:T(8,128)S(1)} %reshape.158), kind=kOutput, calls=%fused_computation.4 | convolution fusion | flops 1133936640 | bytes 6000896 | tf_op jit(solution)/shard_map/dot_general | solution.py:25
  123.7 0.9 slice_bitcast_fusion
  124.8 0.4 fusion.60
  125.2 2.6 %fusion.106 = (f32[8,6,40]{2,1,0:T(8,128)S(1)}, f32[8,6,40,40]{2,3,1,0:T(8,128)}) fusion(bf16[40,8,6,128]{3,1,2,0:T(8,128)(2,1)S(1)} %get-tuple-element.7, bf16[40,8,6,128]{3,1,2,0:T(8,128)(2,1)} %get-tuple-element.6), kind=kOutput, calls=%fused_computation.123 | convolution fusion | flops 19891240 | bytes 1297920 | tf_op jit(solution)/shard_map/sub | solution.py:40
  127.8 2.6 %fusion.48 = bf16[40,8,6,128]{3,0,2,1:T(8,128)(2,1)} fusion(bf16[40,8,6,128]{3,1,2,0:T(8,128)(2,1)} %fusion.43, f32[8,6,40,40]{2,3,1,0:T(8,128)} %get-tuple-element.11, f32[8,6,40]{2,1,0:T(8,128)S(1)} %get-tuple-element.10), kind=kOutput, calls=%fused_computation.55 | convolution fusion | flops 20060160 | bytes 1297920 | tf_op jit(solution)/shard_map/bhlm,lbhe->mbhe/dot_general | solution.py:69
  130.3 3.0 %fusion.47 = bf16[40,8,6,128]{3,0,2,1:T(8,128)(2,1)} fusion(f32[8,6,40,40]{2,3,1,0:T(8,128)S(1)} %fusion.60, bf16[40,8,6,128]{3,1,2,0:T(8,128)(2,1)} %get-tuple-element.6, f32[8,6,40,40]{2,3,1,0:T(8,128)} %get-tuple-element.11, f32[8,6,40]{2,1,0:T(8,128)S(1)} %get-tuple-element.10), kind=kOutput, calls=%fused_computation.54 | convolution fusion | flops 20446120 | bytes 1605120 | tf_op jit(solution)/shard_map/bhlm,lbhe->mbhe/dot_general | solution.py:77
  133.3 2.9 %fusion.46 = bf16[40,8,6,128]{3,0,2,1:T(8,128)(2,1)} fusion(f32[8,6,40,40]{2,3,1,0:T(8,128)S(1)} %fusion.60, bf16[40,8,6,128]{3,1,2,0:T(8,128)(2,1)S(1)} %get-tuple-element.7, f32[8,6,40,40]{2,3,1,0:T(8,128)} %get-tuple-element.11, f32[8,6,40]{2,1,0:T(8,128)S(1)} %get-tuple-element.10), kind=kOutput, calls=%fused_computation.53 | convolution fusion | flops 20446120 | bytes 1605120 | tf_op jit(solution)/shard_map/bhlm,mbhe->lbhe/dot_general | solution.py:74
  136.3 1.2 copy.183
  137.4 1.4 copy_bitcast_fusion.1
  138.8 3.5 %multiply_reduce_fusion.3 = (f32[40,8]{1,0:T(8,128)S(1)}, f32[40,8,768]{2,1,0:T(8,128)S(1)}) fusion(f32[40,8,768]{2,1,0:T(8,128)S(1)} %bitcast.136, f32[768]{0:T(1024)S(1)} %copy-done.7, bf16[768,2304]{1,0:T(8,128)(2,1)} %all-gather.9.cloned.1.call-done, bf16[40,8,768]{2,1,0:T(8,128)(2,1)S(1)} %get-tuple-element.16, ...), kind=kOutput, calls=%fused_computation.69 | convolution fusion | flops 1137622784 | bytes 6983936 | tf_op jit(solution)/shard_map/dot_general | solution.py:83
  142.3 0.3 add_convert_fusion.1
  142.6 19.6 %all_to_all.84 = bf16[40,8,768]{2,1,0:T(8,128)(2,1)S(1)} all-to-all(bf16[40,8,768]{2,1,0:T(8,128)(2,1)S(1)} %add_convert_fusion.1), channel_id=1, replica_groups=mesh['tr'=4,'gz'=8] {'gz'}, dimensions={0} | all-to-all | bytes 983040 | tf_op jit(solution)/shard_map/all_to_all | solution.py:126
  162.3 0.6 fusion.44
  162.9 0.6 copy-done.9
  163.5 1.2 fusion.51
  164.7 1.5 fusion.79
  166.2 2.7 %fusion.49 = bf16[40,8,768]{2,1,0:T(8,128)(2,1)} fusion(f32[40,6,8,8]{2,3,1,0:T(8,128)S(1)} %fusion.79, bf16[40,8,2304]{2,1,0:T(8,128)(2,1)} %copy-done.5, f32[40,6,8,8]{2,3,1,0:T(8,128)S(1)} %copy-done.10, f32[40,6,8]{2,1,0:T(8,128)} %copy-done.11), kind=kOutput, calls=%fused_computation.56 | convolution fusion | flops 4287367 | bytes 5242880 | tf_op jit(solution)/shard_map/bhlm,bmhe->blhe/dot_general | solution.py:74
  168.9 2.6 %fusion.50 = bf16[40,8,768]{2,1,0:T(8,128)(2,1)} fusion(f32[40,6,8,8]{2,3,1,0:T(8,128)S(1)} %fusion.79, bf16[40,8,2304]{2,1,0:T(8,128)(2,1)} %copy-done.5, f32[40,6,8,8]{2,3,1,0:T(8,128)S(1)} %copy-done.10, f32[40,6,8]{2,1,0:T(8,128)} %copy-done.11), kind=kOutput, calls=%fused_computation.57 | convolution fusion | flops 4287367 | bytes 5242880 | tf_op jit(solution)/shard_map/bhlm,blhe->bmhe/dot_general | solution.py:77
  171.5 3.9 %multiply_reduce_fusion.2 = (f32[40,8]{1,0:T(8,128)S(1)}, f32[40,8,768]{2,1,0:T(8,128)S(1)}) fusion(f32[40,8,768]{2,1,0:T(8,128)S(1)} %reshape.140, f32[768]{0:T(1024)S(1)} %copy-done.8, bf16[768,2304]{1,0:T(8,128)(2,1)} %all-gather.5.cloned.1.call-done, bf16[40,8,768]{2,1,0:T(8,128)(2,1)} %fusion.51, bf16[40,8,768]{2,1,0:T(8,128)(2,1)} %fusion.50, ...), kind=kOutput, calls=%fused_computation.67 | convolution fusion | flops 1137622784 | bytes 6983936 | tf_op jit(solution)/shard_map/dot_general | solution.py:83
  175.4 0.3 add_convert_fusion
  175.9 10.9 %all_to_all.85 = bf16[5,8,8,768]{3,1,0,2:T(8,128)(2,1)S(1)} all-to-all(bf16[5,8,8,768]{3,1,0,2:T(8,128)(2,1)S(1)} %copy.139), channel_id=1, replica_groups=mesh['tr'=4,'gz'=8] {'tr'}, dimensions={2} | all-to-all | bytes 983040 | tf_op jit(solution)/shard_map/all_to_all | solution.py:130
  186.7 1.2 copy.140
  (47 shorter events, 1.3 us)
Async XLA Ops:
  6.5 2.8 %copy-start.2 = (bf16[5,32,2,768]{3,2,1,0:T(2,128)(2,1)S(1)}, bf16[5,32,2,768]{3,2,1,0:T(2,128)(2,1)}, u32[]{:S(2)}) copy-start(bf16[5,32,2,768]{3,2,1,0:T(2,128)(2,1)} %param.8) | copy-start | bytes 1474564
  6.5 45.4 %all-gather.5.cloned.1.call-start = ((), (), s32[]{:S(2)}) async-start(), calls=%async_computation.6 | async-start | bytes 4423680 | tf_op jit(solution)/shard_map/all_gather | solution.py:106
  7.3 61.8 %all-gather.7.cloned.1.call-start = ((), (), s32[]{:S(2)}) async-start(), calls=%async_computation.7 | async-start | bytes 1474560 | tf_op jit(solution)/shard_map/all_gather | solution.py:107
  8.0 80.1 %all-gather.11.cloned.1.call-start = ((), (), s32[]{:S(2)}) async-start(), calls=%async_computation.9 | async-start | bytes 1474560 | tf_op jit(solution)/shard_map/all_gather | solution.py:111
  8.7 5.9 %copy-start.3 = (bf16[5,32,2,768]{3,2,1,0:T(2,128)(2,1)S(1)}, bf16[5,32,2,768]{3,2,1,0:T(2,128)(2,1)}, u32[]{:S(2)}) copy-start(bf16[5,32,2,768]{3,2,1,0:T(2,128)(2,1)} %param.9) | copy-start | bytes 1474564
  8.8 111.5 %all-gather.9.cloned.1.call-start = ((), (), s32[]{:S(2)}) async-start(), calls=%async_computation.8 | async-start | bytes 4423680 | tf_op jit(solution)/shard_map/all_gather | solution.py:110
  10.5 14.5 %all-to-all-start.2 = ((bf16[5,32,2,768]{3,2,0,1:T(2,128)(2,1)}), bf16[5,32,2,768]{3,2,0,1:T(2,128)(2,1)S(1)}, u32[]{:S(2)}, u32[]{:S(2)}) async-start(bf16[5,32,2,768]{3,2,0,1:T(2,128)(2,1)} %copy.114), calls=%async_computation.2 | async-start | bytes 983040 | tf_op jit(solution)/shard_map/all_to_all | solution.py:114
  25.0 17.5 %all-to-all-start = ((bf16[5,32,2,768]{3,2,0,1:T(2,128)(2,1)}), bf16[5,32,2,768]{3,2,0,1:T(2,128)(2,1)S(1)}, u32[]{:S(2)}, u32[]{:S(2)}) async-start(bf16[5,32,2,768]{3,2,0,1:T(2,128)(2,1)} %copy.109), calls=%async_computation | async-start | bytes 983040 | tf_op jit(solution)/shard_map/all_to_all | solution.py:115
  43.5 29.4 %all-to-all-start.1 = ((bf16[5,64,768]{2,0,1:T(8,128)(2,1)}), bf16[5,64,768]{2,0,1:T(8,128)(2,1)S(1)}, u32[]{:S(2)}, u32[]{:S(2)}) async-start(bf16[5,64,768]{2,0,1:T(8,128)(2,1)} %bitcast.2), calls=%async_computation.1 | async-start | bytes 1572864 | tf_op jit(solution)/shard_map/all_to_all | solution.py:118
  50.8 1.1 copy-start.8
  55.3 1.8 copy-start.5
  57.1 14.6 %copy-start.11 = (f32[40,6,8]{2,1,0:T(8,128)}, f32[40,6,8]{2,1,0:T(8,128)S(1)}, u32[]{:S(2)}) copy-start(f32[40,6,8]{2,1,0:T(8,128)S(1)} %get-tuple-element.8) | copy-start | bytes 23044
  72.9 26.1 %all-to-all-start.3 = ((bf16[5,64,768]{2,0,1:T(8,128)(2,1)}), bf16[5,64,768]{2,0,1:T(8,128)(2,1)S(1)}, u32[]{:S(2)}, u32[]{:S(2)}) async-start(bf16[5,64,768]{2,0,1:T(8,128)(2,1)} %copy.121), calls=%async_computation.3 | async-start | bytes 1572864 | tf_op jit(solution)/shard_map/all_to_all | solution.py:122
  78.5 20.7 %copy-start = (bf16[8,5,8,768]{3,2,1,0:T(8,128)(2,1)}, bf16[8,5,8,768]{3,2,1,0:T(8,128)(2,1)S(1)}, u32[]{:S(2)}) copy-start(bf16[8,5,8,768]{3,2,1,0:T(8,128)(2,1)S(1)} %copy.113) | copy-start | bytes 1474564
  90.7 29.6 %copy-start.7 = (f32[768]{0:T(1024)S(1)}, f32[768]{0:T(1024)}, u32[]{:S(2)}) copy-start(f32[768]{0:T(1024)} %param.13) | copy-start | bytes 9220
  123.7 1.1 copy-start.4
  138.8 3.5 %copy-start.1 = (bf16[8,5,8,768]{3,2,1,0:T(8,128)(2,1)S(1)}, bf16[8,5,8,768]{3,2,1,0:T(8,128)(2,1)}, u32[]{:S(2)}) copy-start(bf16[8,5,8,768]{3,2,1,0:T(8,128)(2,1)} %copy-done) | copy-start | bytes 1474564
  142.6 19.7 %copy-start.6 = (bf16[768,768]{1,0:T(8,128)(2,1)S(1)}, bf16[768,768]{1,0:T(8,128)(2,1)}, u32[]{:S(2)}) copy-start(bf16[768,768]{1,0:T(8,128)(2,1)} %all-gather.7.cloned.1.call-done) | copy-start | bytes 3538948
  162.3 1.2 copy-start.9
  162.3 1.2 copy-start.12
  164.7 1.5 copy-start.10
Sparse Core Ops, SparseCore 0:
  8.9 40.0 all-gather.4
  50.5 18.4 all-gather.6
  70.6 17.4 all-gather.10
  89.5 30.7 all-gather.8
where the time goes:
time: 195 us; the launch traced here: 194 us
  waiting for transfers between devices  75.3 us (39%)
  matrix products  41.2 us (21%)
  blocking collectives  30.5 us (16%)
  starting transfers between devices  20.6 us (11%)
  between operations  13.4 us (7%)
  local copies, waits for them, and re-layouts  11.4 us (6%)
    all_gather x1, waiting for transfers between devices, per_device(): lax.all_gather(wqkv_z, 'tr', axis=0, tiled=True)  20.7 us
    all_to_all x1, blocking collectives, per_device(): lax.all_to_all(grad_columns, 'gz', split_axis=0, concat_axis=1, tiled=True)  19.6 us
    all_to_all x1, waiting for transfers between devices, per_device(): lax.all_to_all(cotangent, 'tr', split_axis=1, concat_axis=2, tiled=True)  13.1 us
    all_gather x1, waiting for transfers between devices, per_device(): lax.all_gather(wo_x, 'tr', axis=0, tiled=True)  11.9 us
    all_to_all x1, blocking collectives, per_device(): lax.all_to_all(result_lines, 'tr', split_axis=2, concat_axis=1, tiled=True)  10.9 us
    all_gather x1, waiting for transfers between devices, per_device(): lax.all_gather(wo_z, 'tr', axis=0, tiled=True)  9.53 us
    all_to_all x1, waiting for transfers between devices, per_device(): lax.all_to_all(tokens, 'tr', split_axis=1, concat_axis=2, tiled=True)  9.19 us
    all_to_all x1, waiting for transfers between devices, per_device(): lax.all_to_all(mid_lines.reshape(flat), 'gz', split_axis=1, concat_axis=0...  8.26 us
  transfers between devices with their start and end apart: 8, of which 6 were waited for; matrix products, arithmetic and copies ran while one was open for 9% of the time, Pallas kernels for 0%

commit v1 on v0

--- a/solution.py
+++ b/solution.py
@@ -5,6 +5,24 @@
 from jax.sharding import PartitionSpec as P
 
 H = 6
+
+
+def collect(value, axis, dim):
+    ways, here, step = (lax.axis_size(axis), lax.axis_index(axis), value.shape[dim])
+    shape = [n * ways if d == dim else n for d, n in enumerate(value.shape)]
+    full = lax.dynamic_update_slice_in_dim(
+        jnp.zeros(shape, value.dtype), value, here * step, axis=dim
+    )
+    going_up = going_down = value
+    for far in range(1, ways // 2 + 1):
+        going_up = lax.ppermute(going_up, axis, [(d, (d + 1) % ways) for d in range(ways)])
+        full = lax.dynamic_update_slice_in_dim(full, going_up, (here - far) % ways * step, axis=dim)
+        if 2 * far < ways:
+            going_down = lax.ppermute(going_down, axis, [(d, (d - 1) % ways) for d in range(ways)])
+            full = lax.dynamic_update_slice_in_dim(
+                full, going_down, (here + far) % ways * step, axis=dim
+            )
+    return full
 
 
 def head_split(packed, index, model_width):
@@ -107,7 +125,7 @@
         lax.all_gather(wo_x, "tr", axis=0, tiled=True),
     )
     full_in_z, full_out_z = (
-        lax.all_gather(wqkv_z, "tr", axis=0, tiled=True),
+        collect(wqkv_z, "tr", 0),
         lax.all_gather(wo_z, "tr", axis=0, tiled=True),
     )
     width = tokens.shape[-1]

time: 195 us -> 188 us (0.964)
  waiting for transfers between devices: 75.3 us -> 60.7 us
  local copies, waits for them, and re-layouts: 11.4 us -> 19.7 us
  blocking collectives: 30.5 us -> 28.3 us
    all_to_all x1, waiting for transfers between devices: 9.19 us -> 31.8 us  [per_device(): lax.all_to_all(tokens, 'tr', split_axis=1, concat_axis=2, tiled=True)]
    all_gather x1 -> x0, waiting for transfers between devices: 20.7 us -> none  [per_device(): lax.all_gather(wqkv_z, 'tr', axis=0, tiled=True)]
    all_gather x1, waiting for transfers between devices: 11.9 us -> 0.02 us  [per_device(): lax.all_gather(wo_x, 'tr', axis=0, tiled=True)]
    all_gather x1, waiting for transfers between devices: 9.53 us -> 0.02 us  [per_device(): lax.all_gather(wo_z, 'tr', axis=0, tiled=True)]
    dynamic_update_slice x0 -> x4, local copies, waits for them, and re-layouts: none -> 7.48 us  [the longest x2 4.33 us: collect(): lax.dynamic_update_slice_in_dim(full, going_up, (here - far) % ways * ste...]
    all_to_all x1, waiting for transfers between devices: 0.01 us -> 7.32 us  [per_device(): lax.all_to_all(cot_lines.reshape(flat), 'gz', split_axis=1, concat_axis=0...]
    all_to_all x1, waiting for transfers between devices: 13.1 us -> 6.43 us  [per_device(): lax.all_to_all(cotangent, 'tr', split_axis=1, concat_axis=2, tiled=True)]
    all_to_all x1, waiting for transfers between devices: 8.26 us -> 13 us  [per_device(): lax.all_to_all(mid_lines.reshape(flat), 'gz', split_axis=1, concat_axis=0...]
  transfers between devices with their start and end apart: 8 -> 10, of which waited for: 6 -> 4; matrix products, arithmetic and copies ran while one was open for 9% -> 16% of each run, Pallas kernels for 0% -> 0%
where the time goes in v1:
time: 188 us; the launch traced here: 187 us
  waiting for transfers between devices  60.7 us (32%)
  matrix products  42.4 us (23%)
  blocking collectives  28.3 us (15%)
  starting transfers between devices  20.4 us (11%)
  local copies, waits for them, and re-layouts  19.7 us (10%)
  between operations  13.5 us (7%)
  other arithmetic  1.89 us (1%)
    all_to_all x1, waiting for transfers between devices, per_device(): lax.all_to_all(tokens, 'tr', split_axis=1, concat_axis=2, tiled=True)  31.8 us
    all_to_all x1, blocking collectives, per_device(): lax.all_to_all(grad_columns, 'gz', split_axis=0, concat_axis=1, tiled=True)  17.5 us
    all_to_all x1, waiting for transfers between devices, per_device(): lax.all_to_all(mid_lines.reshape(flat), 'gz', split_axis=1, concat_axis=0...  13 us
    all_to_all x1, blocking collectives, per_device(): lax.all_to_all(result_lines, 'tr', split_axis=2, concat_axis=1, tiled=True)  10.9 us
    dot_general x2, matrix products, recompute(): jnp.dot(normed, w_in, preferred_element_type=jnp.float32)  7.87 us
    all_to_all x1, waiting for transfers between devices, per_device(): lax.all_to_all(cot_lines.reshape(flat), 'gz', split_axis=1, concat_axis=0...  7.32 us
    all_to_all x1, starting transfers between devices, per_device(): lax.all_to_all(cot_lines.reshape(flat), 'gz', split_axis=1, concat_axis=0...  7.09 us
    all_to_all x1, waiting for transfers between devices, per_device(): lax.all_to_all(cotangent, 'tr', split_axis=1, concat_axis=2, tiled=True)  6.43 us
  transfers between devices with their start and end apart: 10, of which 4 were waited for; matrix products, arithmetic and copies ran while one was open for 16% of the time, Pallas kernels for 0%

profile of v1, /device:TPU:0, one launch (start us, length us, event | category | flops | bytes accessed | tf_op | source)
XLA Modules:
  0.0 186.9 jit_solution(5418886847737771807)
XLA Ops:
  6.5 0.7 all-gather.4.cloned.1.call-update
  7.3 0.7 all-gather.6.cloned.1.call-update
  8.0 0.5 collective-permute-start
  8.5 2.0 %collective-permute-start.1 = (bf16[192,2304]{1,0:T(8,128)(2,1)}, bf16[192,2304]{1,0:T(8,128)(2,1)}, u32[]{:S(2)}, u32[]{:S(2)}) collective-permute-start(bf16[192,2304]{1,0:T(8,128)(2,1)} %param.14), channel_id=1, source_target_pairs={{0,24},{8,0},{16,8},{24,16},{1,25},{9,1},{17,9},{25,17},{2,26},{10... | collective-permute-start | bytes 2654216 | tf_op jit(solution)/shard_map/ppermute | solution.py:21
  10.5 2.1 %copy.114 = bf16[5,32,2,768]{3,2,0,1:T(2,128)(2,1)} copy(bf16[5,32,2,768]{3,2,1,0:T(2,128)(2,1)} %param.8) | data formatting | bytes 983040 | tf_op args[0]
  12.7 3.5 %all-to-all-start.2 = ((bf16[5,32,2,768]{3,2,0,1:T(2,128)(2,1)}), bf16[5,32,2,768]{3,2,0,1:T(2,128)(2,1)S(1)}, u32[]{:S(2)}, u32[]{:S(2)}) async-start(bf16[5,32,2,768]{3,2,0,1:T(2,128)(2,1)} %copy.114), calls=%async_computation.2 | async-start | bytes 983040 | tf_op jit(solution)/shard_map/all_to_all | solution.py:132
  16.2 0.7 all-gather.8.cloned.1.call-update
  16.9 1.1 copy.109
  18.1 2.0 %broadcast_in_dim.2 = bf16[768,2304]{1,0:T(8,128)(2,1)} broadcast(bf16[]{:T(256)} %constant.45.clone.1), dimensions={} | broadcast | bytes 3538946 | tf_op jit(solution)/shard_map/broadcast_in_dim | solution.py:14
  20.1 1.0 constant_dynamic-update-slice_fusion.3
  21.1 31.8 %all-to-all-done.2 = bf16[5,32,2,768]{3,2,0,1:T(2,128)(2,1)S(1)} async-done(((bf16[5,32,2,768]{3,2,0,1:T(2,128)(2,1)}), bf16[5,32,2,768]{3,2,0,1:T(2,128)(2,1)S(1)}, u32[]{:S(2)}, u32[]{:S(2)}) %all-to-all-start.2) | async-done | bytes 491552 | tf_op jit(solution)/shard_map/all_to_all | solution.py:132
  52.9 3.5 %all-to-all-start = ((bf16[5,32,2,768]{3,2,0,1:T(2,128)(2,1)}), bf16[5,32,2,768]{3,2,0,1:T(2,128)(2,1)S(1)}, u32[]{:S(2)}, u32[]{:S(2)}) async-start(bf16[5,32,2,768]{3,2,0,1:T(2,128)(2,1)} %copy.109), calls=%async_computation | async-start | bytes 983040 | tf_op jit(solution)/shard_map/all_to_all | solution.py:133
  56.4 0.4 copy_bitcast_fusion
  56.8 0.7 reshape.140
  57.4 0.6 multiply_reduce_fusion.4
  58.4 6.4 %all-to-all-done = bf16[5,32,2,768]{3,2,0,1:T(2,128)(2,1)S(1)} async-done(((bf16[5,32,2,768]{3,2,0,1:T(2,128)(2,1)}), bf16[5,32,2,768]{3,2,0,1:T(2,128)(2,1)S(1)}, u32[]{:S(2)}, u32[]{:S(2)}) %all-to-all-start) | async-done | bytes 491552 | tf_op jit(solution)/shard_map/all_to_all | solution.py:133
  64.8 1.0 copy.144
  65.9 7.1 %all-to-all-start.1 = ((bf16[5,64,768]{2,0,1:T(8,128)(2,1)}), bf16[5,64,768]{2,0,1:T(8,128)(2,1)S(1)}, u32[]{:S(2)}, u32[]{:S(2)}) async-start(bf16[5,64,768]{2,0,1:T(8,128)(2,1)} %bitcast.2), calls=%async_computation.1 | async-start | bytes 1572864 | tf_op jit(solution)/shard_map/all_to_all | solution.py:136
  73.0 2.1 %constant_dynamic-update-slice_fusion.2 = bf16[768,2304]{1,0:T(8,128)(2,1)} fusion(bf16[768,2304]{1,0:T(8,128)(2,1)} %constant_dynamic-update-slice_fusion.3, bf16[192,2304]{1,0:T(8,128)(2,1)} %collective-permute-done, s32[]{:T(128)S(6)} %select_n.29), kind=kLoop, calls=%fused_computation.110 | loop fusion | bytes 1769476 | tf_op jit(solution)/shard_map/dynamic_update_slice | solution.py:19
  75.2 4.5 %convolution_convert_fusion.1 = bf16[40,8,2304]{2,1,0:T(8,128)(2,1)} fusion(bf16[768,2304]{1,0:T(8,128)(2,1)} %all-gather.4.cloned.1.call-done, f32[40,8,768]{2,1,0:T(8,128)S(1)} %reshape.140, f32[768]{0:T(1024)S(1)} %copy-done.8, f32[40,8]{1,0:T(8,128)S(1)} %copy.119), kind=kOutput, calls=%fused_computation.5 | convolution fusion | flops 1133936640 | bytes 6000896 | tf_op jit(solution)/shard_map/dot_general | solution.py:43
  79.7 2.0 %fusion.105 = (f32[40,6,8]{2,1,0:T(8,128)S(1)}, f32[40,6,8,8]{2,3,1,0:T(8,128)S(1)}) fusion(bf16[40,8,2304]{2,1,0:T(8,128)(2,1)} %convolution_convert_fusion.1), kind=kOutput, calls=%fused_computation.126 | convolution fusion | flops 3978247 | bytes 1052160 | tf_op jit(solution)/shard_map/sub | solution.py:58
  81.7 2.7 %fusion.40 = bf16[40,8,768]{2,1,0:T(8,128)(2,1)S(1)} fusion(f32[40,8,768]{2,1,0:T(8,128)S(1)} %reshape.140, bf16[768,768]{1,0:T(8,128)(2,1)} %all-gather.6.cloned.1.call-done, bf16[40,8,2304]{2,1,0:T(8,128)(2,1)} %convolution_convert_fusion.1, f32[40,6,8,8]{2,3,1,0:T(8,128)S(1)} %get-tuple-element.9, f32[40,6,8]{2,1,0:T(8,128)S(1)} %get-tuple-element.8), kind=kOutput, calls=%fused_computation.38 | convolution fusion | flops 382187520 | bytes 3214848 | tf_op jit(solution)/shard_map/dot_general | solution.py:72
  84.5 1.2 copy.121
  85.7 7.3 %all-to-all-done.1 = bf16[5,64,768]{2,0,1:T(8,128)(2,1)S(1)} async-done(((bf16[5,64,768]{2,0,1:T(8,128)(2,1)}), bf16[5,64,768]{2,0,1:T(8,128)(2,1)S(1)}, u32[]{:S(2)}, u32[]{:S(2)}) %all-to-all-start.1) | async-done | bytes 491552 | tf_op jit(solution)/shard_map/all_to_all | solution.py:136
  93.0 3.7 %all-to-all-start.3 = ((bf16[5,64,768]{2,0,1:T(8,128)(2,1)}), bf16[5,64,768]{2,0,1:T(8,128)(2,1)S(1)}, u32[]{:S(2)}, u32[]{:S(2)}) async-start(bf16[5,64,768]{2,0,1:T(8,128)(2,1)} %copy.121), calls=%async_computation.3 | async-start | bytes 1572864 | tf_op jit(solution)/shard_map/all_to_all | solution.py:140
  96.7 2.1 %constant_dynamic-update-slice_fusion.1 = bf16[768,2304]{1,0:T(8,128)(2,1)} fusion(bf16[768,2304]{1,0:T(8,128)(2,1)} %constant_dynamic-update-slice_fusion.2, bf16[192,2304]{1,0:T(8,128)(2,1)} %collective-permute-done.1, s32[]{:T(128)S(6)} %select_n.31), kind=kLoop, calls=%fused_computation.109 | loop fusion | bytes 1769476 | tf_op jit(solution)/shard_map/dynamic_update_slice | solution.py:22
  99.0 2.6 %fusion.43 = bf16[40,8,6,128]{3,1,2,0:T(8,128)(2,1)} fusion(bf16[40,8,768]{2,1,0:T(8,128)(2,1)S(1)} %bitcast.138, bf16[768,768]{1,0:T(8,128)(2,1)} %all-gather.8.cloned.1.call-done), kind=kOutput, calls=%fused_computation.50 | convolution fusion | flops 377733120 | bytes 2162688 | tf_op jit(solution)/shard_map/dot_general | solution.py:82
  101.7 2.2 %constant_dynamic-update-slice_fusion = bf16[768,2304]{1,0:T(8,128)(2,1)} fusion(bf16[768,2304]{1,0:T(8,128)(2,1)} %constant_dynamic-update-slice_fusion.1, bf16[192,2304]{1,0:T(8,128)(2,1)} %collective-permute-done.2, s32[]{:T(128)S(6)} %select_n.33), kind=kLoop, calls=%fused_computation.108 | loop fusion | bytes 1769476 | tf_op jit(solution)/shard_map/dynamic_update_slice | solution.py:19
  103.9 13.0 %all-to-all-done.3 = bf16[5,64,768]{2,0,1:T(8,128)(2,1)S(1)} async-done(((bf16[5,64,768]{2,0,1:T(8,128)(2,1)}), bf16[5,64,768]{2,0,1:T(8,128)(2,1)S(1)}, u32[]{:S(2)}, u32[]{:S(2)}) %all-to-all-start.3) | async-done | bytes 491552 | tf_op jit(solution)/shard_map/all_to_all | solution.py:140
  117.5 3.4 %convolution_convert_fusion = bf16[40,8,2304]{2,1,0:T(8,128)(2,1)S(1)} fusion(bf16[768,2304]{1,0:T(8,128)(2,1)} %constant_dynamic-update-slice_fusion, f32[40,8,768]{2,1,0:T(8,128)S(1)} %bitcast.135, f32[768]{0:T(1024)S(1)} %copy-done.7, f32[40,8]{1,0:T(8,128)S(1)} %reshape.158), kind=kOutput, calls=%fused_computation.4 | convolution fusion | flops 1133936640 | bytes 6000896 | tf_op jit(solution)/shard_map/dot_general | solution.py:43
  120.8 1.1 slice_bitcast_fusion
  121.9 0.4 fusion.60
  122.4 2.8 %fusion.106 = (f32[8,6,40]{2,1,0:T(8,128)S(1)}, f32[8,6,40,40]{2,3,1,0:T(8,128)}) fusion(bf16[40,8,6,128]{3,1,2,0:T(8,128)(2,1)} %get-tuple-element.7, bf16[40,8,6,128]{3,1,2,0:T(8,128)(2,1)} %get-tuple-element.6), kind=kOutput, calls=%fused_computation.127 | convolution fusion | flops 19891240 | bytes 1297920 | tf_op jit(solution)/shard_map/sub | solution.py:58
  125.1 3.1 %fusion.46 = bf16[40,8,6,128]{3,0,2,1:T(8,128)(2,1)} fusion(f32[8,6,40,40]{2,3,1,0:T(8,128)S(1)} %fusion.60, bf16[40,8,6,128]{3,1,2,0:T(8,128)(2,1)} %get-tuple-element.7, f32[8,6,40,40]{2,3,1,0:T(8,128)} %get-tuple-element.11, f32[8,6,40]{2,1,0:T(8,128)S(1)} %get-tuple-element.10), kind=kOutput, calls=%fused_computation.53 | convolution fusion | flops 20446120 | bytes 1605120 | tf_op jit(solution)/shard_map/bhlm,mbhe->lbhe/dot_general | solution.py:92
  128.2 3.0 %fusion.47 = bf16[40,8,6,128]{3,0,2,1:T(8,128)(2,1)} fusion(f32[8,6,40,40]{2,3,1,0:T(8,128)S(1)} %fusion.60, bf16[40,8,6,128]{3,1,2,0:T(8,128)(2,1)} %get-tuple-element.6, f32[8,6,40,40]{2,3,1,0:T(8,128)} %get-tuple-element.11, f32[8,6,40]{2,1,0:T(8,128)S(1)} %get-tuple-element.10), kind=kOutput, calls=%fused_computation.54 | convolution fusion | flops 20446120 | bytes 1605120 | tf_op jit(solution)/shard_map/bhlm,lbhe->mbhe/dot_general | solution.py:95
  131.2 1.8 fusion.48
  133.4 3.4 %multiply_reduce_fusion.3 = (f32[40,8]{1,0:T(8,128)S(1)}, f32[40,8,768]{2,1,0:T(8,128)S(1)}) fusion(f32[40,8,768]{2,1,0:T(8,128)S(1)} %bitcast.136, f32[768]{0:T(1024)S(1)} %copy-done.7, bf16[768,2304]{1,0:T(8,128)(2,1)} %constant_dynamic-update-slice_fusion, bf16[40,8,768]{2,1,0:T(8,128)(2,1)S(1)} %get-tuple-element.16, ...), kind=kOutput, calls=%fused_computation.69 | convolution fusion | flops 1137622784 | bytes 6983936 | tf_op jit(solution)/shard_map/dot_general | solution.py:101
  136.8 0.3 add_convert_fusion.1
  137.2 17.5 %all_to_all.84 = bf16[40,8,768]{2,1,0:T(8,128)(2,1)S(1)} all-to-all(bf16[40,8,768]{2,1,0:T(8,128)(2,1)S(1)} %add_convert_fusion.1), channel_id=1, replica_groups=mesh['tr'=4,'gz'=8] {'gz'}, dimensions={0} | all-to-all | bytes 983040 | tf_op jit(solution)/shard_map/all_to_all | solution.py:144
  154.7 0.6 fusion.44
  155.3 1.4 fusion.79
  156.7 3.2 %fusion.49 = bf16[40,8,768]{2,1,0:T(8,128)(2,1)} fusion(f32[40,6,8,8]{2,3,1,0:T(8,128)S(1)} %fusion.79, bf16[40,8,2304]{2,1,0:T(8,128)(2,1)} %convolution_convert_fusion.1, f32[40,6,8,8]{2,3,1,0:T(8,128)} %copy-done.9, f32[40,6,8]{2,1,0:T(8,128)S(1)} %copy-done.11), kind=kOutput, calls=%fused_computation.56 | convolution fusion | flops 4287367 | bytes 4321280 | tf_op jit(solution)/shard_map/bhlm,bmhe->blhe/dot_general | solution.py:92
  159.9 3.1 %fusion.50 = bf16[40,8,768]{2,1,0:T(8,128)(2,1)} fusion(f32[40,6,8,8]{2,3,1,0:T(8,128)S(1)} %fusion.79, bf16[40,8,2304]{2,1,0:T(8,128)(2,1)} %convolution_convert_fusion.1, f32[40,6,8,8]{2,3,1,0:T(8,128)} %copy-done.9, f32[40,6,8]{2,1,0:T(8,128)S(1)} %copy-done.11), kind=kOutput, calls=%fused_computation.57 | convolution fusion | flops 4287367 | bytes 4321280 | tf_op jit(solution)/shard_map/bhlm,blhe->bmhe/dot_general | solution.py:95
  163.0 1.8 fusion.51
  164.8 0.6 copy-done.5
  165.3 2.6 %multiply_reduce_fusion.2 = (f32[40,8]{1,0:T(8,128)S(1)}, f32[40,8,768]{2,1,0:T(8,128)S(1)}) fusion(f32[40,8,768]{2,1,0:T(8,128)S(1)} %reshape.140, f32[768]{0:T(1024)S(1)} %copy-done.8, bf16[768,2304]{1,0:T(8,128)(2,1)S(1)} %copy-done.5, bf16[40,8,768]{2,1,0:T(8,128)(2,1)S(1)} %fusion.51, bf16[40,8,768]{2,1,0:T(8,128)(2,1)} %fusion.50, ...), kind=kOutput, calls=%fused_computation.67 | convolution fusion | flops 1137622784 | bytes 6983936 | tf_op jit(solution)/shard_map/dot_general | solution.py:101
  168.4 10.9 %all_to_all.85 = bf16[5,8,8,768]{3,1,0,2:T(8,128)(2,1)S(1)} all-to-all(bf16[5,8,8,768]{3,1,0,2:T(8,128)(2,1)S(1)} %copy.139), channel_id=1, replica_groups=mesh['tr'=4,'gz'=8] {'tr'}, dimensions={2} | all-to-all | bytes 983040 | tf_op jit(solution)/shard_map/all_to_all | solution.py:148
  179.3 1.2 copy.140
  (53 shorter events, 2.0 us)
Async XLA Ops:
  6.5 10.4 %copy-start.1 = (bf16[5,32,2,768]{3,2,1,0:T(2,128)(2,1)S(1)}, bf16[5,32,2,768]{3,2,1,0:T(2,128)(2,1)}, u32[]{:S(2)}) copy-start(bf16[5,32,2,768]{3,2,1,0:T(2,128)(2,1)} %param.9) | copy-start | bytes 1474564
  6.5 68.6 %all-gather.4.cloned.1.call-start = ((), (), s32[]{:S(2)}) async-start(), calls=%async_computation.6 | async-start | bytes 4423680 | tf_op jit(solution)/shard_map/all_gather | solution.py:124
  7.3 74.5 %all-gather.6.cloned.1.call-start = ((), (), s32[]{:S(2)}) async-start(), calls=%async_computation.7 | async-start | bytes 1474560 | tf_op jit(solution)/shard_map/all_gather | solution.py:125
  8.0 64.9 %collective-permute-start = (bf16[192,2304]{1,0:T(8,128)(2,1)}, bf16[192,2304]{1,0:T(8,128)(2,1)}, u32[]{:S(2)}, u32[]{:S(2)}) collective-permute-start(bf16[192,2304]{1,0:T(8,128)(2,1)} %param.14), channel_id=1, source_target_pairs={{0,8},{8,16},{16,24},{24,0},{1,9},{9,17},{17,25},{25,1},{2,10},{10... | collective-permute-start | bytes 2654216 | tf_op jit(solution)/shard_map/ppermute | solution.py:18
  8.5 88.2 %collective-permute-start.1 = (bf16[192,2304]{1,0:T(8,128)(2,1)}, bf16[192,2304]{1,0:T(8,128)(2,1)}, u32[]{:S(2)}, u32[]{:S(2)}) collective-permute-start(bf16[192,2304]{1,0:T(8,128)(2,1)} %param.14), channel_id=1, source_target_pairs={{0,24},{8,0},{16,8},{24,16},{1,25},{9,1},{17,9},{25,17},{2,26},{10... | collective-permute-start | bytes 2654216 | tf_op jit(solution)/shard_map/ppermute | solution.py:21
  12.7 40.3 %all-to-all-start.2 = ((bf16[5,32,2,768]{3,2,0,1:T(2,128)(2,1)}), bf16[5,32,2,768]{3,2,0,1:T(2,128)(2,1)S(1)}, u32[]{:S(2)}, u32[]{:S(2)}) async-start(bf16[5,32,2,768]{3,2,0,1:T(2,128)(2,1)} %copy.114), calls=%async_computation.2 | async-start | bytes 983040 | tf_op jit(solution)/shard_map/all_to_all | solution.py:132
  16.2 82.9 %all-gather.8.cloned.1.call-start = ((), (), s32[]{:S(2)}) async-start(), calls=%async_computation.8 | async-start | bytes 1474560 | tf_op jit(solution)/shard_map/all_gather | solution.py:129
  18.1 2.0 %copy-start = (bf16[192,2304]{1,0:T(8,128)(2,1)S(1)}, bf16[192,2304]{1,0:T(8,128)(2,1)}, u32[]{:S(2)}) copy-start(bf16[192,2304]{1,0:T(8,128)(2,1)} %param.14) | copy-start | bytes 2654212
  52.9 11.9 %all-to-all-start = ((bf16[5,32,2,768]{3,2,0,1:T(2,128)(2,1)}), bf16[5,32,2,768]{3,2,0,1:T(2,128)(2,1)S(1)}, u32[]{:S(2)}, u32[]{:S(2)}) async-start(bf16[5,32,2,768]{3,2,0,1:T(2,128)(2,1)} %copy.109), calls=%async_computation | async-start | bytes 983040 | tf_op jit(solution)/shard_map/all_to_all | solution.py:133
  65.9 9.3 %copy-start.8 = (f32[768]{0:T(1024)S(1)}, f32[768]{0:T(1024)}, u32[]{:S(2)}) copy-start(f32[768]{0:T(1024)} %param.10) | copy-start | bytes 9220
  65.9 27.1 %all-to-all-start.1 = ((bf16[5,64,768]{2,0,1:T(8,128)(2,1)}), bf16[5,64,768]{2,0,1:T(8,128)(2,1)S(1)}, u32[]{:S(2)}, u32[]{:S(2)}) async-start(bf16[5,64,768]{2,0,1:T(8,128)(2,1)} %bitcast.2), calls=%async_computation.1 | async-start | bytes 1572864 | tf_op jit(solution)/shard_map/all_to_all | solution.py:136
  73.0 28.7 %collective-permute-start.2 = (bf16[192,2304]{1,0:T(8,128)(2,1)}, bf16[192,2304]{1,0:T(8,128)(2,1)}, u32[]{:S(2)}, u32[]{:S(2)}) collective-permute-start(bf16[192,2304]{1,0:T(8,128)(2,1)} %collective-permute-done), channel_id=1, source_target_pairs={{0,8},{8,16},{16,24},{24,0},{1,9},{9,17},{17,25},{25,1},{2,10},{10... | collective-permute-start | bytes 2654216 | tf_op jit(solution)/shard_map/ppermute | solution.py:18
  81.7 2.8 %copy-start.9 = (f32[40,6,8,8]{2,3,1,0:T(8,128)}, f32[40,6,8,8]{2,3,1,0:T(8,128)S(1)}, u32[]{:S(2)}) copy-start(f32[40,6,8,8]{2,3,1,0:T(8,128)S(1)} %get-tuple-element.9) | copy-start | bytes 184324
  81.7 2.8 %copy-start.10 = (f32[40,6,8]{2,1,0:T(8,128)}, f32[40,6,8]{2,1,0:T(8,128)S(1)}, u32[]{:S(2)}) copy-start(f32[40,6,8]{2,1,0:T(8,128)S(1)} %get-tuple-element.8) | copy-start | bytes 23044
  93.0 23.9 %all-to-all-start.3 = ((bf16[5,64,768]{2,0,1:T(8,128)(2,1)}), bf16[5,64,768]{2,0,1:T(8,128)(2,1)S(1)}, u32[]{:S(2)}, u32[]{:S(2)}) async-start(bf16[5,64,768]{2,0,1:T(8,128)(2,1)} %copy.121), calls=%async_computation.3 | async-start | bytes 1572864 | tf_op jit(solution)/shard_map/all_to_all | solution.py:140
  103.9 13.6 %copy-start.7 = (f32[768]{0:T(1024)S(1)}, f32[768]{0:T(1024)}, u32[]{:S(2)}) copy-start(f32[768]{0:T(1024)} %param.13) | copy-start | bytes 9220
  120.8 1.1 copy-start.3
  131.2 1.8 copy-start.2
  131.2 2.0 %copy-start.4 = (bf16[40,8,6,128]{3,0,2,1:T(8,128)(2,1)S(1)}, bf16[40,8,6,128]{3,0,2,1:T(8,128)(2,1)}, u32[]{:S(2)}) copy-start(bf16[40,8,6,128]{3,0,2,1:T(8,128)(2,1)} %fusion.47) | copy-start | bytes 1474564
  137.1 17.5 %copy-start.6 = (bf16[768,768]{1,0:T(8,128)(2,1)S(1)}, bf16[768,768]{1,0:T(8,128)(2,1)}, u32[]{:S(2)}) copy-start(bf16[768,768]{1,0:T(8,128)(2,1)} %all-gather.6.cloned.1.call-done) | copy-start | bytes 3538948
  154.7 2.0 %copy-start.11 = (f32[40,6,8]{2,1,0:T(8,128)S(1)}, f32[40,6,8]{2,1,0:T(8,128)}, u32[]{:S(2)}) copy-start(f32[40,6,8]{2,1,0:T(8,128)} %copy-done.10) | copy-start | bytes 23044
  163.0 2.3 %copy-start.5 = (bf16[768,2304]{1,0:T(8,128)(2,1)S(1)}, bf16[768,2304]{1,0:T(8,128)(2,1)}, u32[]{:S(2)}) copy-start(bf16[768,2304]{1,0:T(8,128)(2,1)} %all-gather.4.cloned.1.call-done) | copy-start | bytes 10616836
Sparse Core Ops, SparseCore 0:
  8.9 47.7 all-gather.3
  58.2 19.5 all-gather.5
  79.4 17.3 all-gather.7
